TPU v7x, 32 devices: a whole 2x2x4 slice. The times are simulated.
32 devices in a mesh: gx: 4 (over y, core), gy: 4 (over z), gz: 2 (over x).
Axes of the slice: x: 2, y: 2, z: 4, core: 2. Of those that a mesh axis runs over, the one named last changes fastest.
Arguments:
- initial_thermal_state: float32 [256, 128, 256], P('gx', 'gy', 'gz'), may hold values from -6 to 6
- thermal_spread_rate: float32 [256, 128, 256], P('gx', 'gy', 'gz'), may hold values from 0.25 to 4
- yz_skew_factor: bfloat16 [256, 128, 256], P('gx', 'gy', 'gz'), may hold values from -1 to 1
Outputs:
- known_source_vector: float32 [256, 128, 256], P('gx', 'gy', 'gz')
- half_step: float32 [256, 128, 256], P('gx', 'gy', 'gz')
All inputs are finite; a program needn't handle non-finite values.
Results may differ from a plain program's by a relative error of at most 0.0003.
Values sent between devices are 32-bit elements; how exact they have to be, the bound alone decides.
A program may use at most 64 MiB of HBM per device.

v0:
```python
import functools
import math

import jax
import jax.numpy as jnp
from jax import lax
from jax.experimental import pallas as pl
from jax.experimental.pallas import tpu as pltpu
from jax.sharding import PartitionSpec as P

ratio_x = 4096.0
ratio_y = 0.2
ratio_z = 0.2
ratio_mix = 0.25
VMEM1 = 61 * 1024 * 1024 + 512 * 1024
VMEM2 = 48 * 1024 * 1024
MESH = pl.DeviceIdType.MESH


def link(first, second):
    t1, z1, c1 = first
    t2, z2, c2 = second
    k1 = t1 / (1.0 + z1 * c2)
    k2 = t2 / (1.0 + z1 * c2)
    return (k1 * t2, z2 + k2 * t2 * z1, c1 + k1 * t1 * c2), (k1, k2)


def link_sides(weights, first, first_pq, second, second_pq):
    k1, k2 = weights
    p1, q1 = first_pq
    p2, q2 = second_pq
    return (p2 + k2 * (p1 - first[1] * q2), q1 + k1 * (q2 + second[2] * p1))


def pick(flag, yes, no):
    return tuple(jnp.where(flag, s, t) for s, t in zip(yes, no))


def kernel(
    nx, ny, nz, u_hbm, d_hbm, k_hbm, r_buf, rho, start,
    u_pad, d_pad, skew,
    x_halo, y_send, y_recv, z_send, z_recv, skew_edge,
    map_send, map_recv, pq_send, pq_recv, rel_send, rel_recv,
    load_sem, halo_send, halo_recv, line_send, line_recv,
):
    planes, rows, lanes = u_hbm.shape
    stages = int(math.log2(nx))
    gx, gy, gz = lax.axis_index("gx"), lax.axis_index("gy"), lax.axis_index("gz")
    other_z = 1 - gz
    pitch = rows + 16
    body_rows = pl.ds(8, rows)
    u_flat = u_pad.reshape(planes * pitch, lanes)
    d_flat = d_pad.reshape(planes * pitch, lanes)

    d_load = pltpu.make_async_copy(d_hbm, d_pad.at[:, body_rows, :], load_sem.at[0])
    u_load = pltpu.make_async_copy(u_hbm, u_pad.at[:, body_rows, :], load_sem.at[1])
    k_load = pltpu.make_async_copy(k_hbm, skew, load_sem.at[2])
    d_load.start()
    u_load.start()
    k_load.start()

    barrier = pltpu.get_barrier_semaphore()

    def greet(x, y, z):
        pl.semaphore_signal(barrier, inc=1, device_id=(x, y, z), device_id_type=MESH)

    partners = [gx + (1 << s) - 2 * (1 << s) * ((gx // (1 << s)) % 2) for s in range(stages)]
    for x in partners:
        greet(x, gy, gz)
    greet(gx, gy, other_z)

    @pl.when(gx > 0)
    def _():
        greet(gx - 1, gy, gz)

    @pl.when(gy > 0)
    def _():
        greet(gx, gy - 1, gz)
        greet(gx, gy - 1, other_z)

    @pl.when(gy < ny - 1)
    def _():
        greet(gx, gy + 1, gz)
        greet(gx, gy + 1, other_z)

    one = jnp.int32(1)
    zero = jnp.int32(0)
    awaited = (
        stages + 1
        + jnp.where(gx < nx - 1, one, zero)
        + 2 * jnp.where(gy > 0, one, zero)
        + 2 * jnp.where(gy < ny - 1, one, zero)
    )

    def remote(src, dst, send, recv, x, y, z):
        return pltpu.make_async_remote_copy(
            src_ref=src, dst_ref=dst, send_sem=send, recv_sem=recv,
            device_id=(x, y, z), device_id_type=MESH,
        )

    x_copy = remote(
        d_hbm.at[planes - 1], x_halo, halo_send.at[0], halo_recv.at[0], gx + 1, gy, gz
    )
    up_copy = remote(y_send.at[0], y_recv.at[1], halo_send.at[1], halo_recv.at[1], gx, gy - 1, gz)
    down_copy = remote(y_send.at[1], y_recv.at[0], halo_send.at[2], halo_recv.at[2], gx, gy + 1, gz)
    z_copy = remote(
        z_send, z_recv.at[pl.ds(8, rows), :], halo_send.at[3], halo_recv.at[3], gx, gy, other_z
    )
    up_corner = remote(
        z_send.at[pl.ds(0, 8), :], z_recv.at[pl.ds(8 + rows, 8), :],
        halo_send.at[4], halo_recv.at[4], gx, gy - 1, other_z,
    )
    down_corner = remote(
        z_send.at[pl.ds(rows - 8, 8), :], z_recv.at[pl.ds(0, 8), :],
        halo_send.at[5], halo_recv.at[5], gx, gy + 1, other_z,
    )

    pl.semaphore_wait(barrier, awaited)

    @pl.when(gx < nx - 1)
    def _():
        x_copy.start()

    @pl.when(gx == 0)
    def _():
        x_halo[...] = jnp.zeros((rows, lanes), jnp.float32)

    @pl.when(gy == 0)
    def _():
        y_recv[0] = jnp.zeros((2, planes, lanes), jnp.float32)
        z_recv[0:8, :] = jnp.zeros((8, lanes), jnp.float32)

    @pl.when(gy == ny - 1)
    def _():
        y_recv[1] = jnp.zeros((2, planes, lanes), jnp.float32)
        z_recv[8 + rows : 16 + rows, :] = jnp.zeros((8, lanes), jnp.float32)

    lane = lax.broadcasted_iota(jnp.int32, (rows, lanes), 1)
    edge = jnp.where(gz == 0, jnp.int32(lanes - 1), zero)

    d_load.wait()
    u_load.wait()
    for field, flat in enumerate((u_flat, d_flat)):
        y_send[0, field] = flat[pl.ds(8, planes, stride=pitch), :]
        y_send[1, field] = flat[pl.ds(7 + rows, planes, stride=pitch), :]

    @pl.when(gy > 0)
    def _():
        up_copy.start()

    @pl.when(gy < ny - 1)
    def _():
        down_copy.start()

    def gather_edge(i, acc):
        heat = pltpu.roll(u_pad[i, 8 : 8 + rows, :], lax.rem(i - edge + lanes, lanes), 1)
        diff = pltpu.roll(d_pad[i, 8 : 8 + rows, :], lax.rem(i + planes - edge + lanes, lanes), 1)
        acc = jnp.where(lane == i, heat, acc)
        return jnp.where(lane == i + planes, diff, acc)

    zeros = jnp.zeros((rows, lanes), jnp.float32)
    ones = jnp.ones((rows, lanes), jnp.float32)
    z_send[...] = lax.fori_loop(0, planes, gather_edge, zeros, unroll=8)
    z_copy.start()

    @pl.when(gy > 0)
    def _():
        up_corner.start()

    @pl.when(gy < ny - 1)
    def _():
        down_corner.start()

    k_load.wait()

    @pl.when(gx > 0)
    def _():
        x_copy.wait_recv()

    def homogeneous(i, state):
        a, b, c, d, before, acc = state
        here = d_pad[i, 8 : 8 + rows, :]
        step = 1.0 / (0.5 * ratio_x * (here + before))
        rho[i] = step
        a = a + step * c
        b = b + step * d
        bend = pltpu.roll(skew[i].astype(jnp.float32), lax.rem(i - edge + lanes, lanes), 1)
        return (a, b, c + a, d + b, here, jnp.where(lane == i, bend, acc))

    a, b, c, d, last, acc = lax.fori_loop(
        0, planes, homogeneous, (ones, zeros, zeros, ones, x_halo[...], zeros), unroll=4
    )
    skew_edge[...] = acc
    closing = jnp.where(gx == nx - 1, 1.0 / (0.5 * ratio_x * last), 0.0)
    inv_d = 1.0 / d
    own = (inv_d, b * inv_d + closing, c * inv_d)

    def post(at, send_buf, recv_buf, values, partner):
        for n, v in enumerate(values):
            send_buf[n] = v
        copy = remote(send_buf, recv_buf, line_send.at[at], line_recv.at[at], partner, gy, gz)
        copy.start()
        return copy

    line = [post(0, map_send.at[0], map_recv.at[0], own, partners[0])]

    @pl.when(gy > 0)
    def _():
        down_copy.wait_recv()
        down_corner.wait_recv()

    @pl.when(gy < ny - 1)
    def _():
        up_copy.wait_recv()
        up_corner.wait_recv()

    z_copy.wait_recv()
    met_heat = z_recv[8 : 8 + rows, :]
    met_diff = pltpu.roll(met_heat, lanes - planes, 1)
    own_edge = z_send[...]
    own_diff = pltpu.roll(own_edge, lanes - planes, 1)
    met_bend = z_recv[9 : 9 + rows, :] - z_recv[7 : 7 + rows, :]
    mix_sign = jnp.where(gz == 0, jnp.float32(ratio_mix), jnp.float32(-ratio_mix))
    edge_term = (0.5 * ratio_z) * (
        own_diff * met_heat + met_diff * (met_heat - own_edge)
    ) + mix_sign * skew_edge[...] * met_bend

    for field, flat in enumerate((u_flat, d_flat)):
        flat[pl.ds(7, planes, stride=pitch), :] = y_recv[0, field]
        flat[pl.ds(8 + rows, planes, stride=pitch), :] = y_recv[1, field]

    first_lane = lane == 0
    last_lane = lane == lanes - 1
    edge_lane = lane == edge

    def source(i, state):
        wp, fp = state
        heat = u_pad[i, 8 : 8 + rows, :]
        diff = d_pad[i, 8 : 8 + rows, :]
        heat_m = u_pad[i, 7 : 7 + rows, :]
        heat_p = u_pad[i, 9 : 9 + rows, :]
        flux_y = (diff + d_pad[i, 9 : 9 + rows, :]) * (heat_p - heat) - (
            diff + d_pad[i, 7 : 7 + rows, :]
        ) * (heat - heat_m)
        next_heat = jnp.where(last_lane, 0.0, pltpu.roll(heat, lanes - 1, 1))
        next_diff = jnp.where(last_lane, 0.0, pltpu.roll(diff, lanes - 1, 1))
        face = (diff + next_diff) * (next_heat - heat)
        before = jnp.where(first_lane, diff * heat, pltpu.roll(face, 1, 1))
        bend = heat_p - heat_m
        mixed = jnp.where(last_lane, 0.0, pltpu.roll(bend, lanes - 1, 1)) - jnp.where(
            first_lane, 0.0, pltpu.roll(bend, 1, 1)
        )
        extra = pltpu.roll(edge_term, lax.rem(edge - i + lanes, lanes), 1)
        side = (
            heat
            + (0.5 * ratio_y) * flux_y
            + (0.5 * ratio_z) * (face - before)
            + ratio_mix * skew[i].astype(jnp.float32) * mixed
            + jnp.where(edge_lane, extra, 0.0)
        )
        r_buf[i] = side
        wp = wp + rho[i] * fp
        return (wp, fp + (wp - side))

    half = planes // 2
    wp, fp = lax.fori_loop(0, half, source, (zeros, zeros), unroll=4)

    flags = [(gx // (1 << s)) % 2 == 1 for s in range(stages)]
    group, right = own, own
    left = (ones, zeros, zeros)
    steps = []
    for s in range(stages - 1):
        if s:
            line.append(post(s, map_send.at[s], map_recv.at[s], group, partners[s]))
        line[s].wait_recv()
        theirs = tuple(map_recv[s, n] for n in range(3))
        first = pick(flags[s], theirs, group)
        second = pick(flags[s], group, theirs)
        joined, weights = link(first, second)
        left_joined, left_weights = link(theirs, left)
        right_joined, right_weights = link(right, theirs)
        steps.append((theirs, first, second, weights, left, left_weights, right, right_weights))
        group = joined
        left = pick(flags[s], left_joined, left)
        right = pick(flags[s], right, right_joined)
    in_right = flags[-1]
    end_weight = group[0] / group[1]
    line.append(post(
        stages - 1, rel_send.at[0], rel_recv.at[0],
        (jnp.where(in_right, group[2] + group[0] * end_weight, group[1]),), partners[-1],
    ))

    wp, fp = lax.fori_loop(half, planes, source, (wp, fp), unroll=4)
    group_pq = (wp - b * inv_d * fp, fp * inv_d)
    left_pq, right_pq = (zeros, zeros), group_pq
    for s in range(stages - 1):
        copy = post(stages + s, pq_send.at[s], pq_recv.at[s], group_pq, partners[s])
        line.append(copy)
        theirs_map, first, second, weights, left_map, left_weights, right_map, right_weights = steps[s]
        copy.wait_recv()
        theirs = tuple(pq_recv[s, n] for n in range(2))
        first_pq = pick(flags[s], theirs, group_pq)
        second_pq = pick(flags[s], group_pq, theirs)
        left_pq = pick(
            flags[s], link_sides(left_weights, theirs_map, theirs, left_map, left_pq), left_pq
        )
        right_pq = pick(
            flags[s], right_pq, link_sides(right_weights, right_map, right_pq, theirs_map, theirs)
        )
        group_pq = link_sides(weights, first, first_pq, second, second_pq)
    copy = post(
        2 * stages - 1, rel_send.at[1], rel_recv.at[1],
        (jnp.where(in_right, group_pq[1] + end_weight * group_pq[0], group_pq[0]),), partners[-1],
    )
    line.append(copy)
    line[stages - 1].wait_recv()
    met = rel_recv[0, 0]
    z0 = jnp.where(in_right, met, 0.0)
    c0 = jnp.where(in_right, 0.0, met)
    left_in = left[0] / (1.0 + z0 * left[2])
    z_in = left[1] + left_in * left[0] * z0
    right_in = jnp.where(in_right, right[0] / right[1], right[0] / (1.0 + right[1] * c0))
    c_in = right[2] + right_in * jnp.where(in_right, right[0], right[0] * c0)
    inv_sum = 1.0 / (1.0 + z_in * c_in)
    copy.wait_recv()
    met = rel_recv[1, 0]
    e0 = jnp.where(in_right, met, 0.0)
    e_in = left_pq[0] + left_in * (e0 - z0 * left_pq[1])
    q_in = right_pq[1] + right_in * jnp.where(in_right, right_pq[0], met + c0 * right_pq[0])
    value = (e_in - z_in * q_in) * inv_sum
    flux = -(c_in * e_in + q_in) * inv_sum

    start[0] = value
    start[1] = flux

    for copy in line:
        copy.wait_send()
    z_copy.wait_send()

    @pl.when(gx < nx - 1)
    def _():
        x_copy.wait_send()

    @pl.when(gy > 0)
    def _():
        up_copy.wait_send()
        up_corner.wait_send()

    @pl.when(gy < ny - 1)
    def _():
        down_copy.wait_send()
        down_corner.wait_send()


def march_kernel(r_buf, rho, start, r_hbm, w_hbm, w_buf, store_sem):
    planes = r_buf.shape[0]
    r_store = pltpu.make_async_copy(r_buf, r_hbm, store_sem.at[0])
    r_store.start()

    def march(i, state):
        value, flux = state
        value = value + rho[i] * flux
        w_buf[i] = value
        return (value, flux + (value - r_buf[i]))

    chunks = 4
    size = planes // chunks
    stores = []
    state = (start[0], start[1])
    for n in range(chunks):
        state = lax.fori_loop(n * size, (n + 1) * size, march, state, unroll=8)
        part = pl.ds(n * size, size)
        store = pltpu.make_async_copy(w_buf.at[part], w_hbm.at[part], store_sem.at[1 + n])
        store.start()
        stores.append(store)
    r_store.wait()
    for store in stores:
        store.wait()


def body(nx, ny, nz, initial_thermal_state, thermal_spread_rate, yz_skew_factor):
    planes, rows, lanes = initial_thermal_state.shape
    stages = int(math.log2(nx))
    f32 = jnp.float32
    block = jax.ShapeDtypeStruct((planes, rows, lanes), f32)
    padded = pltpu.VMEM((planes, rows + 16, lanes), f32)
    full = pltpu.VMEM((planes, rows, lanes), f32)
    plane = pltpu.VMEM((rows, lanes), f32)
    faces = pltpu.VMEM((2, 2, planes, lanes), f32)
    maps = pltpu.VMEM((stages - 1, 3, rows, lanes), f32)
    sides = pltpu.VMEM((stages - 1, 2, rows, lanes), f32)
    relation = pltpu.VMEM((2, 1, rows, lanes), f32)
    r, rho, start = pl.pallas_call(
        functools.partial(kernel, nx, ny, nz),
        out_shape=(full, full, pltpu.VMEM((2, rows, lanes), f32)),
        in_specs=[pl.BlockSpec(memory_space=pltpu.HBM)] * 3,
        out_specs=(pl.BlockSpec(memory_space=pltpu.VMEM),) * 3,
        scratch_shapes=[
            padded, padded, pltpu.VMEM((planes, rows, lanes), jnp.bfloat16),
            plane, faces, faces, plane, pltpu.VMEM((rows + 16, lanes), f32), plane,
            maps, maps, sides, sides, relation, relation,
            pltpu.SemaphoreType.DMA((3,)),
            pltpu.SemaphoreType.DMA((6,)),
            pltpu.SemaphoreType.DMA((6,)),
            pltpu.SemaphoreType.DMA((2 * stages,)),
            pltpu.SemaphoreType.DMA((2 * stages,)),
        ],
        compiler_params=pltpu.CompilerParams(
            collective_id=0, has_side_effects=True, vmem_limit_bytes=VMEM1
        ),
    )(initial_thermal_state, thermal_spread_rate, yz_skew_factor)
    return pl.pallas_call(
        march_kernel,
        out_shape=(block, block),
        in_specs=[pl.BlockSpec(memory_space=pltpu.VMEM)] * 3,
        out_specs=(pl.BlockSpec(memory_space=pl.ANY),) * 2,
        scratch_shapes=[full, pltpu.SemaphoreType.DMA((5,))],
        compiler_params=pltpu.CompilerParams(vmem_limit_bytes=VMEM2),
    )(r, rho, start)


def solution(mesh):
    shape = dict(mesh.shape)
    spec = P("gx", "gy", "gz")
    return jax.shard_map(
        functools.partial(body, shape["gx"], shape["gy"], shape["gz"]),
        mesh=mesh, in_specs=(spec,) * 3, out_specs=(spec,) * 2, check_vma=False,
    )
```

profile of v0, /device:TPU:0, one launch (start us, length us, event | category | flops | bytes accessed | tf_op | source)
XLA Modules:
  0.0 17.1 jit_solution(8920278741190960321)
XLA Ops:
  0.6 15.1 %shard_map.50 = (f32[64,32,128]{2,1,0:T(8,128)S(1)}, f32[64,32,128]{2,1,0:T(8,128)S(1)}, f32[2,32,128]{2,1,0:T(8,128)S(1)}) custom-call(f32[64,32,128]{2,1,0:T(8,128)} %u_hbm.1, f32[64,32,128]{2,1,0:T(8,128)} %d_hbm.1, bf16[64,32,128]{2,1,0:T(8,128)(2,1)} %k_hbm.1), custom_call_target="tpu_custom_call" | custom-call | tf_op jit(solution)/shard_map/pallas_call | solution.py:393
  15.8 1.4 %shard_map.51 = (f32[64,32,128]{2,1,0:T(8,128)}, f32[64,32,128]{2,1,0:T(8,128)}) custom-call(f32[64,32,128]{2,1,0:T(8,128)S(1)} %get-tuple-element.5.r_buf, f32[64,32,128]{2,1,0:T(8,128)S(1)} %get-tuple-element.6.rho, f32[2,32,128]{2,1,0:T(8,128)S(1)} %get-tuple-element.7.start), custom_call_target="tpu_custom_call" | custom-call | tf_op jit(solution)/shard_map/pallas_call | solution.py:412
where the time goes:
time: 17.3 us; the launch traced here: 17.1 us
  Pallas kernels  16.5 us (95%)
  between operations  0.64 us (4%)
    pallas_call x1, Pallas kernels, body(): pl.pallas_call(functools.partial(kernel, nx, ny, nz), out_shape=(full, fu...  15.1 us
    pallas_call x1, Pallas kernels, body(): pl.pallas_call(march_kernel, out_shape=(block, block), in_specs=[pl.Block...  1.35 us

commit v1 on v0

--- a/solution.py
+++ b/solution.py
@@ -115,12 +115,6 @@
         halo_send.at[5], halo_recv.at[5], gx, gy + 1, other_z,
     )
 
-    pl.semaphore_wait(barrier, awaited)
-
-    @pl.when(gx < nx - 1)
-    def _():
-        x_copy.start()
-
     @pl.when(gx == 0)
     def _():
         x_halo[...] = jnp.zeros((rows, lanes), jnp.float32)
@@ -138,44 +132,48 @@
     lane = lax.broadcasted_iota(jnp.int32, (rows, lanes), 1)
     edge = jnp.where(gz == 0, jnp.int32(lanes - 1), zero)
 
-    d_load.wait()
-    u_load.wait()
-    for field, flat in enumerate((u_flat, d_flat)):
+    zeros = jnp.zeros((rows, lanes), jnp.float32)
+    ones = jnp.ones((rows, lanes), jnp.float32)
+
+    def gather_edge(pad, place):
+        def one_plane(i, acc):
+            turned = pltpu.roll(
+                pad[i, 8 : 8 + rows, :], lax.rem(i + place - edge + lanes, lanes), 1
+            )
+            return jnp.where(lane == i + place, turned, acc)
+
+        return one_plane
+
+    acc = zeros
+    for field, load, pad, flat in ((1, d_load, d_pad, d_flat), (0, u_load, u_pad, u_flat)):
+        load.wait()
         y_send[0, field] = flat[pl.ds(8, planes, stride=pitch), :]
         y_send[1, field] = flat[pl.ds(7 + rows, planes, stride=pitch), :]
+        acc = lax.fori_loop(0, planes, gather_edge(pad, field * planes), acc, unroll=8)
+    z_send[...] = acc
+
+    pl.semaphore_wait(barrier, awaited)
+    z_copy.start()
 
     @pl.when(gy > 0)
     def _():
         up_copy.start()
+        up_corner.start()
 
     @pl.when(gy < ny - 1)
     def _():
         down_copy.start()
-
-    def gather_edge(i, acc):
-        heat = pltpu.roll(u_pad[i, 8 : 8 + rows, :], lax.rem(i - edge + lanes, lanes), 1)
-        diff = pltpu.roll(d_pad[i, 8 : 8 + rows, :], lax.rem(i + planes - edge + lanes, lanes), 1)
-        acc = jnp.where(lane == i, heat, acc)
-        return jnp.where(lane == i + planes, diff, acc)
-
-    zeros = jnp.zeros((rows, lanes), jnp.float32)
-    ones = jnp.ones((rows, lanes), jnp.float32)
-    z_send[...] = lax.fori_loop(0, planes, gather_edge, zeros, unroll=8)
-    z_copy.start()
-
-    @pl.when(gy > 0)
-    def _():
-        up_corner.start()
-
-    @pl.when(gy < ny - 1)
-    def _():
         down_corner.start()
 
+    @pl.when(gx < nx - 1)
+    def _():
+        x_copy.start()
+
     k_load.wait()
 
-    @pl.when(gx > 0)
-    def _():
-        x_copy.wait_recv()
+    def bent(i, acc):
+        bend = pltpu.roll(skew[i].astype(jnp.float32), lax.rem(i - edge + lanes, lanes), 1)
+        return jnp.where(lane == i, bend, acc)
 
     def homogeneous(i, state):
         a, b, c, d, before, acc = state
@@ -184,13 +182,22 @@
         rho[i] = step
         a = a + step * c
         b = b + step * d
-        bend = pltpu.roll(skew[i].astype(jnp.float32), lax.rem(i - edge + lanes, lanes), 1)
-        return (a, b, c + a, d + b, here, jnp.where(lane == i, bend, acc))
-
+        return (a, b, c + a, d + b, here, bent(i, acc))
+
+    lead = d_pad[0, 8 : 8 + rows, :]
     a, b, c, d, last, acc = lax.fori_loop(
-        0, planes, homogeneous, (ones, zeros, zeros, ones, x_halo[...], zeros), unroll=4
+        1, planes, homogeneous, (ones, zeros, ones, ones, lead, bent(0, zeros)), unroll=7
     )
     skew_edge[...] = acc
+
+    @pl.when(gx > 0)
+    def _():
+        x_copy.wait_recv()
+
+    step = 1.0 / (0.5 * ratio_x * (lead + x_halo[...]))
+    rho[0] = step
+    b = b + a * step
+    d = d + c * step
     closing = jnp.where(gx == nx - 1, 1.0 / (0.5 * ratio_x * last), 0.0)
     inv_d = 1.0 / d
     own = (inv_d, b * inv_d + closing, c * inv_d)

time: 17.3 us -> 18.1 us (1.046)
  Pallas kernels: 16.5 us -> 17.3 us
    pallas_call x1, Pallas kernels: 15.1 us -> 16 us  [body(): pl.pallas_call(functools.partial(kernel, nx, ny, nz), out_shape=(full, fu...]
where the time goes in v1:
time: 18.1 us; the launch traced here: 18 us
  Pallas kernels  17.3 us (96%)
  between operations  0.64 us (4%)
    pallas_call x1, Pallas kernels, body(): pl.pallas_call(functools.partial(kernel, nx, ny, nz), out_shape=(full, fu...  16 us
    pallas_call x1, Pallas kernels, body(): pl.pallas_call(march_kernel, out_shape=(block, block), in_specs=[pl.Block...  1.35 us

profile of v1, /device:TPU:0, one launch (start us, length us, event | category | flops | bytes accessed | tf_op | source)
XLA Modules:
  0.0 18.0 jit_solution(2456728213916056846)
XLA Ops:
  0.6 16.0 %shard_map.50 = (f32[64,32,128]{2,1,0:T(8,128)S(1)}, f32[64,32,128]{2,1,0:T(8,128)S(1)}, f32[2,32,128]{2,1,0:T(8,128)S(1)}) custom-call(f32[64,32,128]{2,1,0:T(8,128)} %u_hbm.1, f32[64,32,128]{2,1,0:T(8,128)} %d_hbm.1, bf16[64,32,128]{2,1,0:T(8,128)(2,1)} %k_hbm.1), custom_call_target="tpu_custom_call" | custom-call | tf_op jit(solution)/shard_map/pallas_call | solution.py:400
  16.6 1.4 %shard_map.51 = (f32[64,32,128]{2,1,0:T(8,128)}, f32[64,32,128]{2,1,0:T(8,128)}) custom-call(f32[64,32,128]{2,1,0:T(8,128)S(1)} %get-tuple-element.5.r_buf, f32[64,32,128]{2,1,0:T(8,128)S(1)} %get-tuple-element.6.rho, f32[2,32,128]{2,1,0:T(8,128)S(1)} %get-tuple-element.7.start), custom_call_target="tpu_custom_call" | custom-call | tf_op jit(solution)/shard_map/pallas_call | solution.py:419

commit v2 on v1

--- a/solution.py
+++ b/solution.py
@@ -135,21 +135,18 @@
     zeros = jnp.zeros((rows, lanes), jnp.float32)
     ones = jnp.ones((rows, lanes), jnp.float32)
 
-    def gather_edge(pad, place):
-        def one_plane(i, acc):
-            turned = pltpu.roll(
-                pad[i, 8 : 8 + rows, :], lax.rem(i + place - edge + lanes, lanes), 1
-            )
-            return jnp.where(lane == i + place, turned, acc)
-
-        return one_plane
-
-    acc = zeros
-    for field, load, pad, flat in ((1, d_load, d_pad, d_flat), (0, u_load, u_pad, u_flat)):
-        load.wait()
+    def gather_edge(i, acc):
+        heat = pltpu.roll(u_pad[i, 8 : 8 + rows, :], lax.rem(i - edge + lanes, lanes), 1)
+        diff = pltpu.roll(d_pad[i, 8 : 8 + rows, :], lax.rem(i + planes - edge + lanes, lanes), 1)
+        acc = jnp.where(lane == i, heat, acc)
+        return jnp.where(lane == i + planes, diff, acc)
+
+    d_load.wait()
+    u_load.wait()
+    for field, flat in enumerate((u_flat, d_flat)):
         y_send[0, field] = flat[pl.ds(8, planes, stride=pitch), :]
         y_send[1, field] = flat[pl.ds(7 + rows, planes, stride=pitch), :]
-        acc = lax.fori_loop(0, planes, gather_edge(pad, field * planes), acc, unroll=8)
+    acc = lax.fori_loop(0, planes, gather_edge, zeros, unroll=planes)
     z_send[...] = acc
 
     pl.semaphore_wait(barrier, awaited)
@@ -186,7 +183,7 @@
 
     lead = d_pad[0, 8 : 8 + rows, :]
     a, b, c, d, last, acc = lax.fori_loop(
-        1, planes, homogeneous, (ones, zeros, ones, ones, lead, bent(0, zeros)), unroll=7
+        1, planes, homogeneous, (ones, zeros, ones, ones, lead, bent(0, zeros)), unroll=21
     )
     skew_edge[...] = acc
 
@@ -270,7 +267,7 @@
         return (wp, fp + (wp - side))
 
     half = planes // 2
-    wp, fp = lax.fori_loop(0, half, source, (zeros, zeros), unroll=4)
+    wp, fp = lax.fori_loop(0, half, source, (zeros, zeros), unroll=16)
 
     flags = [(gx // (1 << s)) % 2 == 1 for s in range(stages)]
     group, right = own, own
@@ -297,7 +294,7 @@
         (jnp.where(in_right, group[2] + group[0] * end_weight, group[1]),), partners[-1],
     ))
 
-    wp, fp = lax.fori_loop(half, planes, source, (wp, fp), unroll=4)
+    wp, fp = lax.fori_loop(half, planes, source, (wp, fp), unroll=16)
     group_pq = (wp - b * inv_d * fp, fp * inv_d)
     left_pq, right_pq = (zeros, zeros), group_pq
     for s in range(stages - 1):
@@ -375,7 +372,7 @@
     stores = []
     state = (start[0], start[1])
     for n in range(chunks):
-        state = lax.fori_loop(n * size, (n + 1) * size, march, state, unroll=8)
+        state = lax.fori_loop(n * size, (n + 1) * size, march, state, unroll=16)
         part = pl.ds(n * size, size)
         store = pltpu.make_async_copy(w_buf.at[part], w_hbm.at[part], store_sem.at[1 + n])
         store.start()

time: 18.1 us -> 19.1 us (1.055)
  Pallas kernels: 17.3 us -> 18.4 us
    pallas_call x1, Pallas kernels: 16 us -> 17 us  [body(): pl.pallas_call(functools.partial(kernel, nx, ny, nz), out_shape=(full, fu...]
where the time goes in v2:
time: 19.1 us; the launch traced here: 19 us
  Pallas kernels  18.4 us (96%)
  between operations  0.64 us (3%)
    pallas_call x1, Pallas kernels, body(): pl.pallas_call(functools.partial(kernel, nx, ny, nz), out_shape=(full, fu...  17 us
    pallas_call x1, Pallas kernels, body(): pl.pallas_call(march_kernel, out_shape=(block, block), in_specs=[pl.Block...  1.35 us

profile of v2, /device:TPU:0, one launch (start us, length us, event | category | flops | bytes accessed | tf_op | source)
XLA Modules:
  0.0 19.0 jit_solution(363572945127796773)
XLA Ops:
  0.6 17.0 %shard_map.50 = (f32[64,32,128]{2,1,0:T(8,128)S(1)}, f32[64,32,128]{2,1,0:T(8,128)S(1)}, f32[2,32,128]{2,1,0:T(8,128)S(1)}) custom-call(f32[64,32,128]{2,1,0:T(8,128)} %u_hbm.1, f32[64,32,128]{2,1,0:T(8,128)} %d_hbm.1, bf16[64,32,128]{2,1,0:T(8,128)(2,1)} %k_hbm.1), custom_call_target="tpu_custom_call" | custom-call | tf_op jit(solution)/shard_map/pallas_call | solution.py:397
  17.6 1.4 %shard_map.51 = (f32[64,32,128]{2,1,0:T(8,128)}, f32[64,32,128]{2,1,0:T(8,128)}) custom-call(f32[64,32,128]{2,1,0:T(8,128)S(1)} %get-tuple-element.5.r_buf, f32[64,32,128]{2,1,0:T(8,128)S(1)} %get-tuple-element.6.rho, f32[2,32,128]{2,1,0:T(8,128)S(1)} %get-tuple-element.7.start), custom_call_target="tpu_custom_call" | custom-call | tf_op jit(solution)/shard_map/pallas_call | solution.py:416
